TPU v7x, 32 devices: a whole 2x2x4 slice. The times are simulated.
32 devices in a mesh: groups: 2 (over x), rows: 16 (over z, y, core).
Axes of the slice: x: 2, y: 2, z: 4, core: 2. Of those that a mesh axis runs over, the one named last changes fastest.
Arguments:
- features: bfloat16 [3, 256, 8192], P(None, ('groups', 'rows')), parts along dimension 1, may hold values from -6 to 6
- carried: bfloat16 [2, 256, 8192], P(None, ('groups', 'rows')), parts along dimension 1, may hold values from -6 to 6
- flow_shift: int32 [3, 32, 2], P(None, ('groups', 'rows')), parts along dimension 1, may hold values from -8 to 8, as said below
- clip_start: int32 [8], P('groups'), parts along dimension 0, may hold values from 0 to 3
- join_weight: bfloat16 [3, 576, 64], replicated, may hold values from -0.15625 to 0.15625
- res_weight: bfloat16 [4, 3, 192, 64], replicated, may hold values from -0.25 to 0.25
Outputs:
- propagated: bfloat16 [3, 256, 8192], P(None, ('groups', 'rows')), parts along dimension 1
There are 2 independent parts, one for each index of `groups`. A program takes and returns all parts, laid end to end along the dimension named above; an argument that names none is the same for every part. Nothing has to cross between parts.
Inputs may be any that keep to these rules, and one draw needn't show every extreme that they name: `flow_shift`: both ends of the range occur in every draw. `clip_start`: 3 means that the owner begins no clip in these steps.
All inputs are finite; a program needn't handle non-finite values.
Results may differ from a plain program's by a relative error of at most 0.014.
Values may be sent and summed in bfloat16 or wider, within the bound.
A program may use at most 64 MiB of HBM per device.

v0:
```python
import functools

import jax
import jax.numpy as jnp
from jax import lax
from jax.experimental import pallas as pl
from jax.experimental.pallas import tpu as pltpu
from jax.sharding import PartitionSpec as P

SECTIONS = 4
MAXSHIFT = 8
LANES = 128
LEAD = 4


def band_blocks(taps):
    zero = jnp.zeros_like(taps[0])
    blank = jnp.concatenate([zero, zero], axis=1)
    first = jnp.concatenate([taps[0], zero], axis=1)
    second = jnp.concatenate([taps[1], taps[0]], axis=1)
    third = jnp.concatenate([taps[2], taps[1]], axis=1)
    fourth = jnp.concatenate([zero, taps[2]], axis=1)
    return [
        (second, blank),
        (third, first),
        (fourth, second),
        (blank, third),
        (blank, fourth),
        (first, blank),
    ]


def warp(state, shift):
    pairs, rows, lanes = state.shape
    pad = MAXSHIFT // 2
    amount = MAXSHIFT - shift
    moved = jnp.concatenate(
        [
            jnp.zeros((pad, rows, lanes), state.dtype),
            state,
            jnp.zeros((3 * pad, rows, lanes), state.dtype),
        ],
        axis=0,
    )
    step = MAXSHIFT
    while step >= 1:
        bit = (lax.div(amount, 2 * step) % 2 == 1)[None]
        moved = jnp.where(bit, moved[step : moved.shape[0]], moved[: moved.shape[0] - step])
        step //= 2
    moved = moved[: pairs + 1]
    swapped = pltpu.roll(moved, lanes // 2, axis=2)
    low = lax.broadcasted_iota(jnp.int32, (1, rows, lanes), 2) < lanes // 2
    odd = (amount % 2 == 1)[None]
    return jnp.where(odd, jnp.where(low, swapped[:pairs], swapped[1:]), moved[:pairs])


def fill_columns(left_ref, low, high, first):
    groups, rows, lanes = low.shape
    gap = jnp.zeros((1, rows, lanes), low.dtype)
    after = jnp.concatenate([low[1:], gap], axis=0)
    before = jnp.concatenate([gap, high[:-1]], axis=0)
    left_half = lax.broadcasted_iota(jnp.int32, (1, rows, lanes), 2) < lanes // 2
    edge = jnp.where(left_half, after, before)
    window = 16
    for kernel_row in range(3):
        back = (first + kernel_row) % rows
        for part, values in enumerate((low, high, edge)):
            turned = values if back == 0 else pltpu.roll(values, rows - back, axis=1)
            column = (3 * kernel_row + part) * lanes
            left_ref[:, column : column + lanes] = (
                turned[:, :window].reshape(groups * window, lanes).astype(jnp.bfloat16)
            )


def kernel(
    ticks, blocks, row_count, feat, carried, flow, clip, join_w, res_w, out,
    band_w, left, total, sent, above, below, brought, shift_out, shift_in, made, deliver,
    halo_send, halo_recv, feat_send, feat_recv, flow_send, flow_recv, out_send, out_recv, local_sem,
):
    pairs, band_rows = feat.shape[1], feat.shape[2]
    groups = pairs // 2
    channels = join_w.shape[2]
    band_count = row_count // SECTIONS
    me = lax.axis_index("rows")
    spot = lax.rem(me - band_count // 2 + row_count, row_count)
    band = lax.rem(spot, band_count)
    owner = lax.div(spot, band_count)

    def at(offset):
        return {"rows": lax.rem(me + offset % row_count, row_count)}

    offsets = {1, row_count - 1}
    for tick in range(1, ticks):
        offsets |= {(band_count * tick) % row_count, (-band_count * tick) % row_count}
    barrier = pltpu.get_barrier_semaphore()
    for offset in sorted(offsets):
        pl.semaphore_signal(
            barrier, inc=1, device_id=at(offset), device_id_type=pl.DeviceIdType.MESH
        )
    for tick in range(1, ticks):
        for which in range(2):
            shift_out[tick, which] = jnp.full((8, LANES), flow[tick, 0, which], jnp.int32)
    pl.semaphore_wait(barrier, len(offsets))

    pending = []

    def send(source, target, send_sem, recv_sem, offset):
        copy = pltpu.make_async_remote_copy(
            src_ref=source, dst_ref=target, send_sem=send_sem, recv_sem=recv_sem,
            device_id=at(offset), device_id_type=pl.DeviceIdType.MESH,
        )
        copy.start()
        pending.append(copy)
        return copy

    halos = {}

    def send_halo(tick, slot, source):
        halos[tick, slot] = (
            send(source, above.at[tick, slot], halo_send.at[tick, slot, 0],
                 halo_recv.at[tick, slot, 0], 1),
            send(source, below.at[tick, slot], halo_send.at[tick, slot, 1],
                 halo_recv.at[tick, slot, 1], -1),
        )

    def keep(tick):
        begins = clip[lax.rem(owner + tick, SECTIONS)]
        return (jnp.full((8, LANES), begins, jnp.int32) != tick)[None]

    def reset(state, tick):
        return jnp.where(keep(tick), state, 0.0)

    send_halo(0, 2, feat.at[0])
    latest = reset(carried[0].astype(jnp.float32), 0)
    earlier = reset(carried[1].astype(jnp.float32), 0)
    for slot, state in ((1, earlier), (0, latest)):
        shift = jnp.full((8, LANES), flow[0, 0, slot], jnp.int32)
        sent[0, slot] = warp(state, shift).astype(jnp.bfloat16)
        send_halo(0, slot, sent.at[0, slot])
    feats, flows = {}, {}
    for tick in range(1, ticks):
        flows[tick] = send(shift_out.at[tick], shift_in.at[tick], flow_send.at[tick],
                           flow_recv.at[tick], -band_count * tick)
        feats[tick] = send(feat.at[tick], brought.at[tick], feat_send.at[tick],
                           feat_recv.at[tick], -band_count * tick)
    made[0] = latest.astype(jnp.bfloat16)

    for layer in range(3 + 2 * blocks):
        for kernel_row in range(3):
            taps = []
            for column in range(3):
                if layer < 3:
                    start = (column * 3 + layer) * channels
                    taps.append(join_w[kernel_row, start : start + channels, :])
                else:
                    start = column * channels
                    taps.append(res_w[layer - 3, kernel_row, start : start + channels, :])
            for index, (left_part, right_part) in enumerate(band_blocks(taps)):
                start = (kernel_row * 6 + index) * channels
                band_w[layer, start : start + channels, 0:LANES] = left_part
                band_w[layer, start : start + channels, LANES : 2 * LANES] = right_part

    def matmul(layer):
        return jnp.dot(left[...], band_w[layer], preferred_element_type=jnp.float32)

    window = 16
    line = lax.broadcasted_iota(jnp.int32, (1, window, 2 * LANES), 1)
    inside = ((line >= LEAD) | (band > 0)) & (
        (line < LEAD + band_rows) | (band < band_count - 1)
    )

    def settle(values):
        rounded = values.reshape(groups, window, 2 * LANES).astype(jnp.bfloat16)
        return jnp.where(inside, rounded.astype(jnp.float32), 0.0)

    def join(tick, slot, own):
        for copy in halos[tick, slot]:
            copy.wait_recv()
        upper = above[tick, slot].astype(jnp.float32)
        lower = below[tick, slot].astype(jnp.float32)
        upper = jnp.where(band > 0, upper, 0.0)
        lower = jnp.where(band < band_count - 1, lower, 0.0)
        tall = jnp.concatenate([upper, own.astype(jnp.float32), lower], axis=1)
        tall = tall.reshape(groups, 2, 3 * band_rows, LANES)
        fill_columns(left, tall[:, 0], tall[:, 1], band_rows - LEAD - 1)
        return matmul(slot)

    for tick in range(ticks):
        own_feat = feat[0] if tick == 0 else brought[tick]
        total[...] = join(tick, 2, own_feat)
        total[...] += join(tick, 1, sent[tick, 1])
        summed = total[...] + join(tick, 0, sent[tick, 0])
        current = settle(jnp.where(summed >= 0, summed, 0.1 * summed))
        total[...] = current.reshape(groups * window, 2 * LANES)

        if tick + 1 < ticks:
            feats[tick + 1].wait_recv()
            send_halo(tick + 1, 2, brought.at[tick + 1])
            flows[tick + 1].wait_recv()
            earlier = reset(made[tick].astype(jnp.float32), tick + 1)
            sent[tick + 1, 1] = warp(earlier, shift_in[tick + 1, 1]).astype(jnp.bfloat16)
            send_halo(tick + 1, 1, sent.at[tick + 1, 1])

        for block in range(blocks):
            fill_columns(left, current[..., :LANES], current[..., LANES:], window - 1)
            middle = settle(jnp.maximum(matmul(3 + 2 * block), 0.0))
            fill_columns(left, middle[..., :LANES], middle[..., LANES:], window - 1)
            current = settle(total[...] + matmul(4 + 2 * block))
            total[...] = current.reshape(groups * window, 2 * LANES)

        done = pltpu.roll(current, window - LEAD, axis=1)[:, :band_rows]
        state = jnp.stack([done[..., :LANES], done[..., LANES:]], axis=1)
        state = state.reshape(pairs, band_rows, LANES)
        deliver[tick] = state.astype(jnp.bfloat16)
        if tick + 1 < ticks:
            latest = reset(state, tick + 1)
            made[tick + 1] = latest.astype(jnp.bfloat16)
            sent[tick + 1, 0] = warp(latest, shift_in[tick + 1, 0]).astype(jnp.bfloat16)
            send_halo(tick + 1, 0, sent.at[tick + 1, 0])
        if tick == 0:
            home = pltpu.make_async_copy(deliver.at[0], out.at[0], local_sem)
            home.start()
        else:
            halos["out", tick] = (
                send(deliver.at[tick], out.at[tick], out_send.at[tick], out_recv.at[tick],
                     band_count * tick),
            )

    home.wait()
    for copy in pending:
        copy.wait_send()
    for tick in range(1, ticks):
        halos["out", tick][0].wait_recv()


def shards(features, carried, flow_shift, clip_start, join_weight, res_weight):
    ticks, band_rows, wide = features.shape
    channels = join_weight.shape[2]
    blocks = res_weight.shape[0] // 2
    row_count = lax.axis_size("rows")
    pairs = wide // LANES
    groups = pairs // 2

    def paired(array):
        return array.reshape(-1, band_rows, pairs, LANES).transpose(0, 2, 1, 3)

    def vmem(*shape):
        return pltpu.VMEM(shape, jnp.bfloat16)

    whole = pl.BlockSpec(memory_space=pltpu.VMEM)
    scalars = pl.BlockSpec(memory_space=pltpu.SMEM)
    state = (pairs, band_rows, LANES)
    dma = pltpu.SemaphoreType.DMA
    layers = 3 + 2 * blocks
    result = pl.pallas_call(
        functools.partial(kernel, ticks, blocks, row_count),
        out_shape=jax.ShapeDtypeStruct((ticks, *state), jnp.bfloat16),
        in_specs=[whole, whole, scalars, scalars, whole, whole],
        out_specs=pl.BlockSpec(memory_space=pl.ANY),
        scratch_shapes=[
            vmem(layers, 18 * channels, 2 * LANES),
            vmem(groups * 16, 9 * LANES),
            pltpu.VMEM((groups * 16, 2 * LANES), jnp.float32),
            vmem(ticks, 2, *state),
            vmem(ticks, 3, *state),
            vmem(ticks, 3, *state),
            vmem(ticks, *state),
            pltpu.VMEM((ticks, 2, 8, LANES), jnp.int32),
            pltpu.VMEM((ticks, 2, 8, LANES), jnp.int32),
            vmem(ticks, *state),
            vmem(ticks, *state),
            dma((ticks, 3, 2)),
            dma((ticks, 3, 2)),
            dma((ticks,)),
            dma((ticks,)),
            dma((ticks,)),
            dma((ticks,)),
            dma((ticks,)),
            dma((ticks,)),
            dma,
        ],
        compiler_params=pltpu.CompilerParams(
            collective_id=0, has_side_effects=True, vmem_limit_bytes=48 * 1024 * 1024
        ),
    )(paired(features), paired(carried), flow_shift, clip_start, join_weight, res_weight)
    return result.transpose(0, 2, 1, 3).reshape(ticks, band_rows, wide)


def solution(mesh):
    in_specs = (
        P(None, ("groups", "rows"), None),
        P(None, ("groups", "rows"), None),
        P(None, ("groups", "rows"), None),
        P("groups"),
        P(),
        P(),
    )
    out_specs = P(None, ("groups", "rows"), None)
    return jax.shard_map(shards, mesh=mesh, in_specs=in_specs, out_specs=out_specs, check_vma=False)
```

profile of v0, /device:TPU:0, one launch (start us, length us, event | category | flops | bytes accessed | tf_op | source)
XLA Modules:
  0.0 51.8 jit_solution(1527841745958305459)
XLA Ops:
  0.0 0.0 copy-start.3
  0.0 0.8 %copy.7.flow = s32[3,1,2]{2,1,0:T(1,128)S(1)} copy(s32[3,1,2]{0,2,1:T(2,128)} %param.8) | data formatting | bytes 48 | tf_op args[2]
  0.8 1.2 %copy.8.join_w = bf16[3,576,64]{2,1,0:T(8,128)(2,1)S(1)} copy(bf16[3,576,64]{1,2,0:T(8,128)(2,1)} %param.10) | data formatting | bytes 442368 | tf_op args[4]
  2.0 0.0 copy-done.3
  2.0 0.0 copy-start
  2.0 0.0 copy-start.1
  2.0 0.0 copy-start.2
  2.1 0.3 copy.9.res_w
  2.4 0.7 %copy-done = bf16[3,8,8192]{2,1,0:T(8,128)(2,1)S(1)} copy-done((bf16[3,8,8192]{2,1,0:T(8,128)(2,1)S(1)}, bf16[3,8,8192]{2,1,0:T(8,128)(2,1)}, u32[]{:S(2)}) %copy-start) | copy-done | bytes 393240
  3.0 0.1 copy-done.1
  3.1 0.0 copy-done.2
  3.1 47.9 %shard_map.64 = bf16[3,64,8,128]{3,2,1,0:T(8,128)(2,1)S(1)} custom-call(bf16[3,64,8,128]{3,2,1,0:T(8,128)(2,1)S(1)} %bitcast.10, bf16[2,64,8,128]{3,2,1,0:T(8,128)(2,1)S(1)} %bitcast.11, s32[3,1,2]{2,1,0:T(1,128)S(1)} %copy.7.flow, s32[4]{0:T(128)S(1)} %copy-done.2, bf16[3,576,64]{2,1,0:T(8,128)(2,1)S(1)} %copy.8.join_w, bf16[4,3,192,64]{3,2,1,0:T(8,128)(2,1)S(1)} %copy.9.res_w), custom_call_target="tpu_custom_call" | custom-call | tf_op jit(solution)/shard_map/pallas_call | solution.py:255
  51.0 0.7 %copy.11 = bf16[3,8,8192]{2,1,0:T(8,128)(2,1)} copy(bf16[3,8,8192]{2,1,0:T(8,128)(2,1)S(1)} %bitcast.9) | data formatting | bytes 786432
Async XLA Ops:
  0.0 2.0 %copy-start.3 = (bf16[4,3,192,64]{2,3,1,0:T(8,128)(2,1)S(1)}, bf16[4,3,192,64]{2,3,1,0:T(8,128)(2,1)}, u32[]{:S(2)}) copy-start(bf16[4,3,192,64]{2,3,1,0:T(8,128)(2,1)} %param.11) | copy-start | bytes 884740
  2.0 1.0 %copy-start = (bf16[3,8,8192]{2,1,0:T(8,128)(2,1)S(1)}, bf16[3,8,8192]{2,1,0:T(8,128)(2,1)}, u32[]{:S(2)}) copy-start(bf16[3,8,8192]{2,1,0:T(8,128)(2,1)} %param.6) | copy-start | bytes 1179652
  2.0 1.1 %copy-start.1 = (bf16[2,8,8192]{2,1,0:T(8,128)(2,1)S(1)}, bf16[2,8,8192]{2,1,0:T(8,128)(2,1)}, u32[]{:S(2)}) copy-start(bf16[2,8,8192]{2,1,0:T(8,128)(2,1)} %param.7) | copy-start | bytes 786436
  2.0 1.1 %copy-start.2 = (s32[4]{0:T(128)S(1)}, s32[4]{0:T(128)}, u32[]{:S(2)}) copy-start(s32[4]{0:T(128)} %clip.1) | copy-start | bytes 52
where the time goes:
time: 52 us; the launch traced here: 51.8 us
  Pallas kernels  47.9 us (92%)
  local copies, waits for them, and re-layouts  3.8 us (7%)
    pallas_call x1, Pallas kernels, shards(): pl.pallas_call(functools.partial(kernel, ticks, blocks, row_count), out_s...  47.9 us
    unnamed x12, local copies, waits for them, and re-layouts  3.8 us

commit v1 on v0

v1 whole, which is shorter than its diff:
```python
import functools

import jax
import jax.numpy as jnp
from jax import lax
from jax.experimental import pallas as pl
from jax.experimental.pallas import tpu as pltpu
from jax.sharding import PartitionSpec as P

SECTIONS = 4
MAXSHIFT = 8
LANES = 128


def band_blocks(taps):
    zero = jnp.zeros_like(taps[0])
    blank = jnp.concatenate([zero, zero], axis=1)
    first = jnp.concatenate([taps[0], zero], axis=1)
    second = jnp.concatenate([taps[1], taps[0]], axis=1)
    third = jnp.concatenate([taps[2], taps[1]], axis=1)
    fourth = jnp.concatenate([zero, taps[2]], axis=1)
    return [
        (second, blank),
        (third, first),
        (fourth, second),
        (blank, third),
        (blank, fourth),
        (first, blank),
    ]


def turn(values, step):
    return pltpu.roll(values, step % values.shape[1], axis=1)


def warp(state, shift):
    groups = state.shape[1]
    low, high = state[..., :LANES], state[..., LANES:]
    lane = lax.broadcasted_iota(jnp.int32, (1, groups, LANES), 2)
    group = lax.broadcasted_iota(jnp.int32, (1, groups, LANES), 1)
    left_half = lane < LANES // 2
    shift = shift[None]
    quads = lax.shift_right_arithmetic(shift, 2)
    for mask, step in ((quads < 0, -4), ((quads & 2) != 0, 2), ((quads & 1) != 0, 1)):
        low = jnp.where(mask, turn(low, step), low)
        high = jnp.where(mask, turn(high, step), high)
    two = (shift & 2) != 0
    low, high = jnp.where(two, turn(high, 1), low), jnp.where(two, low, high)
    one = (shift & 1) != 0
    low_swap = pltpu.roll(low, LANES // 2, axis=2)
    high_swap = pltpu.roll(high, LANES // 2, axis=2)
    low = jnp.where(one, jnp.where(left_half, turn(high_swap, 1), low_swap), low)
    high = jnp.where(one, jnp.where(left_half, low_swap, high_swap), high)
    origin = group * 4 + lane // (LANES // 2) - shift
    low = jnp.where((origin >= 0) & (origin < 4 * groups), low, 0.0)
    high = jnp.where((origin >= -2) & (origin < 4 * groups - 2), high, 0.0)
    return jnp.concatenate([low, high], axis=-1).astype(jnp.bfloat16)


def edges(values):
    groups = values.shape[1]
    group = lax.broadcasted_iota(jnp.int32, (1, groups, LANES), 1)
    lane = lax.broadcasted_iota(jnp.int32, (1, groups, LANES), 2)
    left_half = lane < LANES // 2
    edge = jnp.where(left_half, turn(values[..., :LANES], -1), turn(values[..., LANES:], 1))
    outside = (left_half & (group == groups - 1)) | ((lane >= LANES // 2) & (group == 0))
    return jnp.where(outside, 0.0, edge).astype(jnp.bfloat16)


def taps_of(main, edge, rows):
    parts = [main[a : a + rows] for a in range(3)] + [edge[a : a + rows] for a in range(3)]
    return jnp.concatenate(parts, axis=-1).reshape(rows * main.shape[1], 9 * LANES)


def kernel(
    ticks, blocks, row_count, feat, carried, flow, clip, join_w, res_w, out,
    band_w, grown, grown_edge, current, current_edge, middle, middle_edge, total, made,
    deliver, shift_out, shift_in,
    halo_send, halo_recv, feat_send, feat_recv, flow_send, flow_recv, out_send, out_recv, local_sem,
):
    band_rows, groups, wide = feat.shape[1:]
    channels = join_w.shape[2]
    rim = 1 + 2 * blocks
    own = pl.ds(rim, band_rows)
    band_count = row_count // SECTIONS
    me = lax.axis_index("rows")
    spot = lax.rem(me - band_count // 2 + row_count, row_count)
    band = lax.rem(spot, band_count)
    owner = lax.div(spot, band_count)

    def at(offset):
        return {"rows": lax.rem(me + offset % row_count, row_count)}

    offsets = {1, row_count - 1}
    for tick in range(1, ticks):
        offsets |= {(band_count * tick) % row_count, (-band_count * tick) % row_count}
    barrier = pltpu.get_barrier_semaphore()
    for offset in sorted(offsets):
        pl.semaphore_signal(
            barrier, inc=1, device_id=at(offset), device_id_type=pl.DeviceIdType.MESH
        )

    pending = []

    def send(source, target, send_sem, recv_sem, offset):
        copy = pltpu.make_async_remote_copy(
            src_ref=source, dst_ref=target, send_sem=send_sem, recv_sem=recv_sem,
            device_id=at(offset), device_id_type=pl.DeviceIdType.MESH,
        )
        copy.start()
        pending.append(copy)
        return copy

    halos = {}

    def send_halo(tick, slot):
        block = grown.at[tick, slot]
        halos[tick, slot] = (
            send(block.at[pl.ds(band_rows, rim)], block.at[pl.ds(0, rim)],
                 halo_send.at[tick, slot, 0], halo_recv.at[tick, slot, 0], 1),
            send(block.at[pl.ds(rim, rim)], block.at[pl.ds(rim + band_rows, rim)],
                 halo_send.at[tick, slot, 1], halo_recv.at[tick, slot, 1], -1),
        )

    def reset(state, tick):
        begins = clip[lax.rem(owner + tick, SECTIONS)]
        keep = jnp.full((groups, wide), begins, jnp.int32) != tick
        return jnp.where(keep[None], state, 0.0)

    grown[0, 2, own] = feat[0]
    for tick in range(1, ticks):
        for which in range(2):
            shift_out[tick, which] = jnp.full((groups, LANES), flow[tick, 0, which], jnp.int32)
    pl.semaphore_wait(barrier, len(offsets))
    send_halo(0, 2)
    for slot in (1, 0):
        state = reset(carried[slot].astype(jnp.float32), 0)
        if slot == 0:
            made[0] = state.astype(jnp.bfloat16)
        shift = jnp.full((groups, LANES), flow[0, 0, slot], jnp.int32)
        grown[0, slot, own] = warp(state, shift)
        send_halo(0, slot)
    feats, flows = {}, {}
    for tick in range(1, ticks):
        flows[tick] = send(shift_out.at[tick], shift_in.at[tick], flow_send.at[tick],
                           flow_recv.at[tick], -band_count * tick)

    def fetch(tick):
        feats[tick] = send(feat.at[tick], grown.at[tick, 2, own], feat_send.at[tick],
                           feat_recv.at[tick], -band_count * tick)

    for layer in range(3 + 2 * blocks):
        for kernel_row in range(3):
            taps = []
            for column in range(3):
                if layer < 3:
                    start = (column * 3 + layer) * channels
                    taps.append(join_w[kernel_row, start : start + channels, :])
                else:
                    start = column * channels
                    taps.append(res_w[layer - 3, kernel_row, start : start + channels, :])
            for index, (left_part, right_part) in enumerate(band_blocks(taps)):
                if index < 4:
                    start = (kernel_row * 4 + index) * channels
                else:
                    start = (12 + kernel_row * 2 + index - 4) * channels
                band_w[layer, start : start + channels, 0:LANES] = left_part
                band_w[layer, start : start + channels, LANES : 2 * LANES] = right_part

    def matmul(main, edge, rows, layer):
        return jnp.dot(
            taps_of(main, edge, rows), band_w[layer], preferred_element_type=jnp.float32
        )

    def clear(refs, rows, margin):
        @pl.when(band == 0)
        def _():
            for ref in refs:
                ref[0:margin] = jnp.zeros((margin, *ref.shape[1:]), ref.dtype)

        @pl.when(band == band_count - 1)
        def _():
            for ref in refs:
                ref[rows - margin : rows] = jnp.zeros((margin, *ref.shape[1:]), ref.dtype)

    def settle(main, edge, values, rows):
        rounded = values.reshape(rows, groups, wide).astype(jnp.bfloat16)
        main[0:rows] = rounded
        edge[0:rows] = edges(rounded.astype(jnp.float32))
        clear((main, edge), rows, (rows - band_rows) // 2)

    most = band_rows + 2 * rim - 2

    def join(tick, slot):
        for copy in halos[tick, slot]:
            copy.wait_recv()
        block = grown.at[tick, slot]
        clear((block,), band_rows + 2 * rim, rim)
        grown_edge[slot] = edges(block[...].astype(jnp.float32))
        return matmul(block, grown_edge.at[slot], most, slot)

    for tick in range(ticks):
        total[...] = join(tick, 2)
        total[...] += join(tick, 1)
        summed = total[...] + join(tick, 0)
        if tick == 0 and ticks > 1:
            fetch(1)
        settle(current, current_edge, jnp.where(summed >= 0, summed, 0.1 * summed), most)
        rows = most
        for block in range(blocks):
            rows -= 2
            hidden = jnp.maximum(matmul(current, current_edge, rows, 3 + 2 * block), 0.0)
            settle(middle, middle_edge, hidden, rows)
            if block == 0 and tick + 1 < ticks:
                flows[tick + 1].wait_recv()
                earlier = reset(made[tick].astype(jnp.float32), tick + 1)
                grown[tick + 1, 1, own] = warp(earlier, shift_in[tick + 1, 1])
                send_halo(tick + 1, 1)
                feats[tick + 1].wait_recv()
                send_halo(tick + 1, 2)
                if tick + 2 < ticks:
                    fetch(tick + 2)
            rows -= 2
            kept = current[2 : 2 + rows].astype(jnp.float32).reshape(rows * groups, wide)
            added = kept + matmul(middle, middle_edge, rows, 4 + 2 * block)
            if block + 1 < blocks:
                settle(current, current_edge, added, rows)
        state = added.reshape(band_rows, groups, wide).astype(jnp.bfloat16)
        deliver[tick] = state
        if tick == 0:
            home = pltpu.make_async_copy(deliver.at[0], out.at[0], local_sem)
            home.start()
        if tick + 1 < ticks:
            latest = reset(state.astype(jnp.float32), tick + 1)
            made[tick + 1] = latest.astype(jnp.bfloat16)
            grown[tick + 1, 0, own] = warp(latest, shift_in[tick + 1, 0])
            send_halo(tick + 1, 0)
        if tick > 0:
            halos["out", tick] = (
                send(deliver.at[tick], out.at[tick], out_send.at[tick], out_recv.at[tick],
                     band_count * tick),
            )

    home.wait()
    for copy in pending:
        copy.wait_send()
    for tick in range(1, ticks):
        halos["out", tick][0].wait_recv()


def shards(features, carried, flow_shift, clip_start, join_weight, res_weight):
    ticks, band_rows, line = features.shape
    channels = join_weight.shape[2]
    blocks = res_weight.shape[0] // 2
    row_count = lax.axis_size("rows")
    wide = 2 * LANES
    groups = line // wide
    rim = 1 + 2 * blocks
    most = band_rows + 2 * rim - 2

    def grouped(array):
        return array.reshape(-1, band_rows, groups, wide)

    def vmem(*shape):
        return pltpu.VMEM(shape, jnp.bfloat16)

    whole = pl.BlockSpec(memory_space=pltpu.VMEM)
    scalars = pl.BlockSpec(memory_space=pltpu.SMEM)
    state = (band_rows, groups, wide)
    dma = pltpu.SemaphoreType.DMA
    result = pl.pallas_call(
        functools.partial(kernel, ticks, blocks, row_count),
        out_shape=jax.ShapeDtypeStruct((ticks, *state), jnp.bfloat16),
        in_specs=[whole, whole, scalars, scalars, whole, whole],
        out_specs=pl.BlockSpec(memory_space=pl.ANY),
        scratch_shapes=[
            vmem(3 + 2 * blocks, 18 * channels, wide),
            vmem(ticks, 3, band_rows + 2 * rim, groups, wide),
            vmem(3, band_rows + 2 * rim, groups, LANES),
            vmem(most, groups, wide),
            vmem(most, groups, LANES),
            vmem(most, groups, wide),
            vmem(most, groups, LANES),
            pltpu.VMEM((most * groups, wide), jnp.float32),
            vmem(ticks, *state),
            vmem(ticks, *state),
            pltpu.VMEM((ticks, 2, groups, LANES), jnp.int32),
            pltpu.VMEM((ticks, 2, groups, LANES), jnp.int32),
            dma((ticks, 3, 2)),
            dma((ticks, 3, 2)),
            dma((ticks,)),
            dma((ticks,)),
            dma((ticks,)),
            dma((ticks,)),
            dma((ticks,)),
            dma((ticks,)),
            dma,
        ],
        compiler_params=pltpu.CompilerParams(
            collective_id=0, has_side_effects=True, vmem_limit_bytes=48 * 1024 * 1024
        ),
    )(grouped(features), grouped(carried), flow_shift, clip_start, join_weight, res_weight)
    return result.reshape(ticks, band_rows, line)


def solution(mesh):
    in_specs = (
        P(None, ("groups", "rows"), None),
        P(None, ("groups", "rows"), None),
        P(None, ("groups", "rows"), None),
        P("groups"),
        P(),
        P(),
    )
    out_specs = P(None, ("groups", "rows"), None)
    return jax.shard_map(shards, mesh=mesh, in_specs=in_specs, out_specs=out_specs, check_vma=False)
```

time: 52 us -> 49.2 us (0.946)
  Pallas kernels: 47.9 us -> 44.4 us
  local copies, waits for them, and re-layouts: 3.8 us -> 4.57 us
    pallas_call x1, Pallas kernels: 47.9 us -> 44.4 us  [shards(): pl.pallas_call(functools.partial(kernel, ticks, blocks, row_count), out_s...]
    reshape x0 -> x1, local copies, waits for them, and re-layouts: none -> 0.93 us  [shards(): return result.reshape(ticks, band_rows, line)]
    unnamed x12 -> x13, local copies, waits for them, and re-layouts: 3.8 us -> 3.64 us
where the time goes in v1:
time: 49.2 us; the launch traced here: 49 us
  Pallas kernels  44.4 us (90%)
  local copies, waits for them, and re-layouts  4.57 us (9%)
    pallas_call x1, Pallas kernels, shards(): pl.pallas_call(functools.partial(kernel, ticks, blocks, row_count), out_s...  44.4 us
    unnamed x13, local copies, waits for them, and re-layouts  3.64 us

profile of v1, /device:TPU:0, one launch (start us, length us, event | category | flops | bytes accessed | tf_op | source)
XLA Modules:
  0.0 49.0 jit_solution(2016556071320436425)
XLA Ops:
  0.0 0.0 copy-start.1
  0.0 0.8 %copy.7.flow = s32[3,1,2]{2,1,0:T(1,128)S(1)} copy(s32[3,1,2]{0,2,1:T(2,128)} %param.8) | data formatting | bytes 48 | tf_op args[2]
  0.8 1.0 %copy.15 = bf16[2,8,32,256]{3,2,1,0:T(8,128)(2,1)S(1)} copy(bf16[2,8,32,256]{3,1,2,0:T(8,128)(2,1)} %bitcast.15) | data formatting | bytes 524288
  1.8 0.0 copy-done.1
  1.8 0.0 copy-start.3
  1.8 0.1 copy.14
  1.9 0.0 copy-start.2
  1.9 0.8 %copy-done.3 = bf16[3,576,64]{1,2,0:T(8,128)(2,1)S(1)} copy-done((bf16[3,576,64]{1,2,0:T(8,128)(2,1)S(1)}, bf16[3,576,64]{1,2,0:T(8,128)(2,1)}, u32[]{:S(2)}) %copy-start.3) | copy-done | bytes 221208
  2.8 0.3 copy.8.join_w
  3.0 0.0 copy-done.2
  3.0 0.0 copy-start
  3.1 0.3 copy.9.res_w
  3.4 0.4 copy-done
  3.7 44.4 %shard_map.64 = bf16[3,8,32,256]{3,2,1,0:T(8,128)(2,1)S(1)} custom-call(bf16[3,8,32,256]{3,2,1,0:T(8,128)(2,1)S(1)} %copy.14, bf16[2,8,32,256]{3,2,1,0:T(8,128)(2,1)S(1)} %copy.15, s32[3,1,2]{2,1,0:T(1,128)S(1)} %copy.7.flow, s32[4]{0:T(128)S(1)} %copy-done, bf16[3,576,64]{2,1,0:T(8,128)(2,1)S(1)} %copy.8.join_w, bf16[4,3,192,64]{3,2,1,0:T(8,128)(2,1)S(1)} %copy.9.res_w), custom_call_target="tpu_custom_call" | custom-call | tf_op jit(solution)/shard_map/pallas_call | solution.py:271
  48.1 0.9 %reshape.11 = bf16[3,8,8192]{2,1,0:T(8,128)(2,1)} reshape(bf16[3,8,32,256]{3,2,1,0:T(8,128)(2,1)S(1)} %shard_map.64) | data formatting | bytes 786432 | tf_op jit(solution)/shard_map/reshape | solution.py:303
Async XLA Ops:
  0.0 1.8 %copy-start.1 = (bf16[3,8,8192]{2,1,0:T(8,128)(2,1)S(1)}, bf16[3,8,8192]{2,1,0:T(8,128)(2,1)}, u32[]{:S(2)}) copy-start(bf16[3,8,8192]{2,1,0:T(8,128)(2,1)} %param.6) | copy-start | bytes 1179652
  1.8 0.9 %copy-start.3 = (bf16[3,576,64]{1,2,0:T(8,128)(2,1)S(1)}, bf16[3,576,64]{1,2,0:T(8,128)(2,1)}, u32[]{:S(2)}) copy-start(bf16[3,576,64]{1,2,0:T(8,128)(2,1)} %param.10) | copy-start | bytes 663556
  1.9 1.1 %copy-start.2 = (bf16[4,3,192,64]{2,3,1,0:T(8,128)(2,1)S(1)}, bf16[4,3,192,64]{2,3,1,0:T(8,128)(2,1)}, u32[]{:S(2)}) copy-start(bf16[4,3,192,64]{2,3,1,0:T(8,128)(2,1)} %param.11) | copy-start | bytes 884740
  3.0 0.7 %copy-start = (s32[4]{0:T(128)S(1)}, s32[4]{0:T(128)}, u32[]{:S(2)}) copy-start(s32[4]{0:T(128)} %clip.1) | copy-start | bytes 52

commit v2 on v1

--- a/solution.py
+++ b/solution.py
@@ -89,7 +89,7 @@
     owner = lax.div(spot, band_count)
 
     def at(offset):
-        return {"rows": lax.rem(me + offset % row_count, row_count)}
+        return {"rows": lax.rem(me + offset, row_count)}
 
     offsets = {1, row_count - 1}
     for tick in range(1, ticks):
@@ -100,27 +100,41 @@
             barrier, inc=1, device_id=at(offset), device_id_type=pl.DeviceIdType.MESH
         )
 
-    pending = []
-
-    def send(source, target, send_sem, recv_sem, offset):
-        copy = pltpu.make_async_remote_copy(
+    def copy_of(source, target, send_sem, recv_sem, offset):
+        return pltpu.make_async_remote_copy(
             src_ref=source, dst_ref=target, send_sem=send_sem, recv_sem=recv_sem,
             device_id=at(offset), device_id_type=pl.DeviceIdType.MESH,
         )
-        copy.start()
-        pending.append(copy)
-        return copy
-
-    halos = {}
+
+    def halo(tick, slot):
+        block = grown.at[tick, slot]
+        return (
+            copy_of(block.at[pl.ds(band_rows, rim)], block.at[pl.ds(0, rim)],
+                    halo_send.at[tick, slot, 0], halo_recv.at[tick, slot, 0], 1),
+            copy_of(block.at[pl.ds(rim, rim)], block.at[pl.ds(rim + band_rows, rim)],
+                    halo_send.at[tick, slot, 1], halo_recv.at[tick, slot, 1], row_count - 1),
+        )
 
     def send_halo(tick, slot):
-        block = grown.at[tick, slot]
-        halos[tick, slot] = (
-            send(block.at[pl.ds(band_rows, rim)], block.at[pl.ds(0, rim)],
-                 halo_send.at[tick, slot, 0], halo_recv.at[tick, slot, 0], 1),
-            send(block.at[pl.ds(rim, rim)], block.at[pl.ds(rim + band_rows, rim)],
-                 halo_send.at[tick, slot, 1], halo_recv.at[tick, slot, 1], -1),
-        )
+        for copy in halo(tick, slot):
+            copy.start()
+
+    def backwards(tick):
+        return row_count - band_count * tick
+
+    def fetched(tick):
+        return copy_of(feat.at[tick], grown.at[tick, 2, own], feat_send.at[tick],
+                       feat_recv.at[tick], backwards(tick))
+
+    def shifts(tick):
+        return copy_of(shift_out.at[tick], shift_in.at[tick], flow_send.at[tick],
+                       flow_recv.at[tick], backwards(tick))
+
+    def delivered(tick):
+        return copy_of(deliver.at[tick], out.at[tick], out_send.at[tick], out_recv.at[tick],
+                       band_count * tick)
+
+    home = pltpu.make_async_copy(deliver.at[0], out.at[0], local_sem)
 
     def reset(state, tick):
         begins = clip[lax.rem(owner + tick, SECTIONS)]
@@ -130,26 +144,22 @@
     grown[0, 2, own] = feat[0]
     for tick in range(1, ticks):
         for which in range(2):
-            shift_out[tick, which] = jnp.full((groups, LANES), flow[tick, 0, which], jnp.int32)
+            shift_out[tick, which] = jnp.full((groups, LANES), flow[0, which, tick], jnp.int32)
     pl.semaphore_wait(barrier, len(offsets))
     send_halo(0, 2)
     for slot in (1, 0):
         state = reset(carried[slot].astype(jnp.float32), 0)
         if slot == 0:
             made[0] = state.astype(jnp.bfloat16)
-        shift = jnp.full((groups, LANES), flow[0, 0, slot], jnp.int32)
+        shift = jnp.full((groups, LANES), flow[0, slot, 0], jnp.int32)
         grown[0, slot, own] = warp(state, shift)
         send_halo(0, slot)
-    feats, flows = {}, {}
     for tick in range(1, ticks):
-        flows[tick] = send(shift_out.at[tick], shift_in.at[tick], flow_send.at[tick],
-                           flow_recv.at[tick], -band_count * tick)
-
-    def fetch(tick):
-        feats[tick] = send(feat.at[tick], grown.at[tick, 2, own], feat_send.at[tick],
-                           feat_recv.at[tick], -band_count * tick)
-
+        shifts(tick).start()
+
+    depth = 18 * channels
     for layer in range(3 + 2 * blocks):
+        base = layer * depth
         for kernel_row in range(3):
             taps = []
             for column in range(3):
@@ -164,13 +174,15 @@
                     start = (kernel_row * 4 + index) * channels
                 else:
                     start = (12 + kernel_row * 2 + index - 4) * channels
-                band_w[layer, start : start + channels, 0:LANES] = left_part
-                band_w[layer, start : start + channels, LANES : 2 * LANES] = right_part
-
-    def matmul(main, edge, rows, layer):
-        return jnp.dot(
-            taps_of(main, edge, rows), band_w[layer], preferred_element_type=jnp.float32
-        )
+                band_w[base + start : base + start + channels, 0:LANES] = left_part
+                band_w[base + start : base + start + channels, LANES : 2 * LANES] = right_part
+
+    if ticks > 1:
+        fetched(1).start()
+
+    def matmul(left, layer, count=1):
+        right = band_w[layer * depth : (layer + count) * depth]
+        return jnp.dot(left, right, preferred_element_type=jnp.float32)
 
     def clear(refs, rows, margin):
         @pl.when(band == 0)
@@ -191,61 +203,76 @@
 
     most = band_rows + 2 * rim - 2
 
-    def join(tick, slot):
-        for copy in halos[tick, slot]:
+    def join_taps(tick, slot):
+        for copy in halo(tick, slot):
             copy.wait_recv()
         block = grown.at[tick, slot]
         clear((block,), band_rows + 2 * rim, rim)
         grown_edge[slot] = edges(block[...].astype(jnp.float32))
-        return matmul(block, grown_edge.at[slot], most, slot)
-
-    for tick in range(ticks):
-        total[...] = join(tick, 2)
-        total[...] += join(tick, 1)
-        summed = total[...] + join(tick, 0)
-        if tick == 0 and ticks > 1:
-            fetch(1)
+        return taps_of(block, grown_edge.at[slot], most)
+
+    def one_tick(tick, nothing):
+        side = jnp.concatenate([join_taps(tick, 1), join_taps(tick, 2)], axis=-1)
+        total[...] = matmul(side, 1, 2)
+        summed = total[...] + matmul(join_taps(tick, 0), 0)
         settle(current, current_edge, jnp.where(summed >= 0, summed, 0.1 * summed), most)
         rows = most
         for block in range(blocks):
             rows -= 2
-            hidden = jnp.maximum(matmul(current, current_edge, rows, 3 + 2 * block), 0.0)
-            settle(middle, middle_edge, hidden, rows)
-            if block == 0 and tick + 1 < ticks:
-                flows[tick + 1].wait_recv()
-                earlier = reset(made[tick].astype(jnp.float32), tick + 1)
-                grown[tick + 1, 1, own] = warp(earlier, shift_in[tick + 1, 1])
-                send_halo(tick + 1, 1)
-                feats[tick + 1].wait_recv()
-                send_halo(tick + 1, 2)
-                if tick + 2 < ticks:
-                    fetch(tick + 2)
+            hidden = matmul(taps_of(current, current_edge, rows), 3 + 2 * block)
+            settle(middle, middle_edge, jnp.maximum(hidden, 0.0), rows)
+            if block == 0:
+                @pl.when(tick + 1 < ticks)
+                def _():
+                    shifts(tick + 1).wait_recv()
+                    earlier = reset(made[tick].astype(jnp.float32), tick + 1)
+                    grown[tick + 1, 1, own] = warp(earlier, shift_in[tick + 1, 1])
+                    send_halo(tick + 1, 1)
+            if block == blocks - 1:
+                @pl.when(tick + 1 < ticks)
+                def _():
+                    fetched(tick + 1).wait_recv()
+                    send_halo(tick + 1, 2)
+
+                @pl.when(tick + 2 < ticks)
+                def _():
+                    fetched(tick + 2).start()
             rows -= 2
             kept = current[2 : 2 + rows].astype(jnp.float32).reshape(rows * groups, wide)
-            added = kept + matmul(middle, middle_edge, rows, 4 + 2 * block)
+            added = kept + matmul(taps_of(middle, middle_edge, rows), 4 + 2 * block)
             if block + 1 < blocks:
                 settle(current, current_edge, added, rows)
-        state = added.reshape(band_rows, groups, wide).astype(jnp.bfloat16)
-        deliver[tick] = state
-        if tick == 0:
-            home = pltpu.make_async_copy(deliver.at[0], out.at[0], local_sem)
-            home.start()
-        if tick + 1 < ticks:
-            latest = reset(state.astype(jnp.float32), tick + 1)
+        deliver[tick] = added.reshape(band_rows, groups, wide).astype(jnp.bfloat16)
+
+        @pl.when(tick + 1 < ticks)
+        def _():
+            latest = reset(deliver[tick].astype(jnp.float32), tick + 1)
             made[tick + 1] = latest.astype(jnp.bfloat16)
             grown[tick + 1, 0, own] = warp(latest, shift_in[tick + 1, 0])
             send_halo(tick + 1, 0)
+
+        @pl.when(tick == 0)
+        def _():
+            home.start()
+
+        @pl.when(tick > 0)
+        def _():
+            delivered(tick).start()
+
+        return nothing
+
+    lax.fori_loop(0, ticks, one_tick, 0)
+
+    home.wait()
+    for tick in range(ticks):
+        for slot in range(3):
+            for copy in halo(tick, slot):
+                copy.wait_send()
         if tick > 0:
-            halos["out", tick] = (
-                send(deliver.at[tick], out.at[tick], out_send.at[tick], out_recv.at[tick],
-                     band_count * tick),
-            )
-
-    home.wait()
-    for copy in pending:
-        copy.wait_send()
-    for tick in range(1, ticks):
-        halos["out", tick][0].wait_recv()
+            shifts(tick).wait_send()
+            fetched(tick).wait_send()
+            delivered(tick).wait_send()
+            delivered(tick).wait_recv()
 
 
 def shards(features, carried, flow_shift, clip_start, join_weight, res_weight):
@@ -274,7 +301,7 @@
         in_specs=[whole, whole, scalars, scalars, whole, whole],
         out_specs=pl.BlockSpec(memory_space=pl.ANY),
         scratch_shapes=[
-            vmem(3 + 2 * blocks, 18 * channels, wide),
+            vmem((3 + 2 * blocks) * 18 * channels, wide),
             vmem(ticks, 3, band_rows + 2 * rim, groups, wide),
             vmem(3, band_rows + 2 * rim, groups, LANES),
             vmem(most, groups, wide),
@@ -299,7 +326,7 @@
         compiler_params=pltpu.CompilerParams(
             collective_id=0, has_side_effects=True, vmem_limit_bytes=48 * 1024 * 1024
         ),
-    )(grouped(features), grouped(carried), flow_shift, clip_start, join_weight, res_weight)
+    )(grouped(features), grouped(carried), flow_shift.transpose(1, 2, 0), clip_start, join_weight, res_weight)
     return result.reshape(ticks, band_rows, line)
 
 

time: 49.2 us -> 46.7 us (0.949)
  Pallas kernels: 44.4 us -> 42.6 us
  local copies, waits for them, and re-layouts: 4.57 us -> 3.84 us
    pallas_call x1, Pallas kernels: 44.4 us -> 42.6 us  [shards(): pl.pallas_call(functools.partial(kernel, ticks, blocks, row_count), out_s...]
    unnamed x13 -> x14, local copies, waits for them, and re-layouts: 3.64 us -> 2.91 us
where the time goes in v2:
time: 46.7 us; the launch traced here: 46.5 us
  Pallas kernels  42.6 us (91%)
  local copies, waits for them, and re-layouts  3.84 us (8%)
    pallas_call x1, Pallas kernels, shards(): pl.pallas_call(functools.partial(kernel, ticks, blocks, row_count), out_s...  42.6 us
    unnamed x14, local copies, waits for them, and re-layouts  2.91 us

profile of v2, /device:TPU:0, one launch (start us, length us, event | category | flops | bytes accessed | tf_op | source)
XLA Modules:
  0.0 46.5 jit_solution(14667571053401512775)
XLA Ops:
  0.0 0.0 copy-start.2
  0.0 1.0 %copy.14 = bf16[2,8,32,256]{3,2,1,0:T(8,128)(2,1)S(1)} copy(bf16[2,8,32,256]{3,1,2,0:T(8,128)(2,1)} %bitcast.17) | data formatting | bytes 524288
  1.1 0.0 copy-done.2
  1.1 0.0 copy-start.4
  1.1 0.1 copy.13
  1.2 0.0 copy-start.3
  1.2 0.8 %copy-done.4 = bf16[3,576,64]{1,2,0:T(8,128)(2,1)S(1)} copy-done((bf16[3,576,64]{1,2,0:T(8,128)(2,1)S(1)}, bf16[3,576,64]{1,2,0:T(8,128)(2,1)}, u32[]{:S(2)}) %copy-start.4) | copy-done | bytes 221208
  2.0 0.2 copy.7.join_w
  2.3 0.0 copy-done.3
  2.3 0.0 copy-start
  2.3 0.0 copy-start.1
  2.3 0.3 copy.8.res_w
  2.6 0.4 copy-done
  3.0 0.0 copy-done.1
  3.0 42.6 %shard_map.64 = bf16[3,8,32,256]{3,2,1,0:T(8,128)(2,1)S(1)} custom-call(bf16[3,8,32,256]{3,2,1,0:T(8,128)(2,1)S(1)} %copy.13, bf16[2,8,32,256]{3,2,1,0:T(8,128)(2,1)S(1)} %copy.14, s32[1,2,3]{2,1,0:T(2,128)S(1)} %bitcast.15, s32[4]{0:T(128)S(1)} %copy-done.1, bf16[3,576,64]{2,1,0:T(8,128)(2,1)S(1)} %copy.7.join_w, bf16[4,3,192,64]{3,2,1,0:T(8,128)(2,1)S(1)} %copy.8.res_w), custom_call_target="tpu_custom_call" | custom-call | tf_op jit(solution)/shard_map/pallas_call | solution.py:298
  45.6 0.9 %reshape.11 = bf16[3,8,8192]{2,1,0:T(8,128)(2,1)} reshape(bf16[3,8,32,256]{3,2,1,0:T(8,128)(2,1)S(1)} %shard_map.64) | data formatting | bytes 786432 | tf_op jit(solution)/shard_map/reshape | solution.py:330
Async XLA Ops:
  0.0 1.1 %copy-start.2 = (bf16[3,8,8192]{2,1,0:T(8,128)(2,1)S(1)}, bf16[3,8,8192]{2,1,0:T(8,128)(2,1)}, u32[]{:S(2)}) copy-start(bf16[3,8,8192]{2,1,0:T(8,128)(2,1)} %param.6) | copy-start | bytes 1179652
  1.1 0.9 %copy-start.4 = (bf16[3,576,64]{1,2,0:T(8,128)(2,1)S(1)}, bf16[3,576,64]{1,2,0:T(8,128)(2,1)}, u32[]{:S(2)}) copy-start(bf16[3,576,64]{1,2,0:T(8,128)(2,1)} %param.10) | copy-start | bytes 663556
  1.2 1.1 %copy-start.3 = (bf16[4,3,192,64]{2,3,1,0:T(8,128)(2,1)S(1)}, bf16[4,3,192,64]{2,3,1,0:T(8,128)(2,1)}, u32[]{:S(2)}) copy-start(bf16[4,3,192,64]{2,3,1,0:T(8,128)(2,1)} %param.11) | copy-start | bytes 884740
  2.3 0.7 %copy-start = (s32[3,1,2]{0,2,1:T(2,128)S(1)}, s32[3,1,2]{0,2,1:T(2,128)}, u32[]{:S(2)}) copy-start(s32[3,1,2]{0,2,1:T(2,128)} %param.8) | copy-start | bytes 76
  2.3 0.7 %copy-start.1 = (s32[4]{0:T(128)S(1)}, s32[4]{0:T(128)}, u32[]{:S(2)}) copy-start(s32[4]{0:T(128)} %clip.1) | copy-start | bytes 52

commit v3 on v2

--- a/solution.py
+++ b/solution.py
@@ -67,14 +67,21 @@
     return jnp.where(outside, 0.0, edge).astype(jnp.bfloat16)
 
 
-def taps_of(main, edge, rows):
-    parts = [main[a : a + rows] for a in range(3)] + [edge[a : a + rows] for a in range(3)]
-    return jnp.concatenate(parts, axis=-1).reshape(rows * main.shape[1], 9 * LANES)
+def lay_taps(left, values, start):
+    rows = values.shape[0] - 2
+    main = values.astype(jnp.bfloat16)
+    edge = edges(values)
+    for a in range(3):
+        column = start + a * 2 * LANES
+        left[0:rows, :, column : column + 2 * LANES] = main[a : a + rows]
+    for a in range(3):
+        column = start + (6 + a) * LANES
+        left[0:rows, :, column : column + LANES] = edge[a : a + rows]
 
 
 def kernel(
     ticks, blocks, row_count, feat, carried, flow, clip, join_w, res_w, out,
-    band_w, grown, grown_edge, current, current_edge, middle, middle_edge, total, made,
+    band_w, grown, joined, current, middle, made,
     deliver, shift_out, shift_in,
     halo_send, halo_recv, feat_send, feat_recv, flow_send, flow_recv, out_send, out_recv, local_sem,
 ):
@@ -180,47 +187,41 @@
     if ticks > 1:
         fetched(1).start()
 
-    def matmul(left, layer, count=1):
-        right = band_w[layer * depth : (layer + count) * depth]
-        return jnp.dot(left, right, preferred_element_type=jnp.float32)
-
-    def clear(refs, rows, margin):
-        @pl.when(band == 0)
-        def _():
-            for ref in refs:
-                ref[0:margin] = jnp.zeros((margin, *ref.shape[1:]), ref.dtype)
-
-        @pl.when(band == band_count - 1)
-        def _():
-            for ref in refs:
-                ref[rows - margin : rows] = jnp.zeros((margin, *ref.shape[1:]), ref.dtype)
-
-    def settle(main, edge, values, rows):
-        rounded = values.reshape(rows, groups, wide).astype(jnp.bfloat16)
-        main[0:rows] = rounded
-        edge[0:rows] = edges(rounded.astype(jnp.float32))
-        clear((main, edge), rows, (rows - band_rows) // 2)
+    def matmul(left, layer, rows, slots=1, start=0):
+        return jnp.dot(
+            left[0:rows, :, start : start + slots * depth].reshape(rows * groups, slots * depth),
+            band_w[layer * depth : (layer + slots) * depth],
+            preferred_element_type=jnp.float32,
+        ).reshape(rows, groups, wide)
+
+    def framed(values, margin):
+        rows = values.shape[0]
+        top = jnp.where(band > 0, values[:margin], 0.0)
+        bottom = jnp.where(band < band_count - 1, values[rows - margin :], 0.0)
+        return jnp.concatenate([top, values[margin : rows - margin], bottom], axis=0)
+
+    def settle(left, values):
+        rounded = values.astype(jnp.bfloat16).astype(jnp.float32)
+        lay_taps(left, framed(rounded, (values.shape[0] - band_rows) // 2), 0)
 
     most = band_rows + 2 * rim - 2
 
-    def join_taps(tick, slot):
+    def lay_join(tick, slot):
         for copy in halo(tick, slot):
             copy.wait_recv()
-        block = grown.at[tick, slot]
-        clear((block,), band_rows + 2 * rim, rim)
-        grown_edge[slot] = edges(block[...].astype(jnp.float32))
-        return taps_of(block, grown_edge.at[slot], most)
+        lay_taps(joined, framed(grown[tick, slot].astype(jnp.float32), rim), slot * depth)
 
     def one_tick(tick, nothing):
-        side = jnp.concatenate([join_taps(tick, 1), join_taps(tick, 2)], axis=-1)
-        total[...] = matmul(side, 1, 2)
-        summed = total[...] + matmul(join_taps(tick, 0), 0)
-        settle(current, current_edge, jnp.where(summed >= 0, summed, 0.1 * summed), most)
+        lay_join(tick, 1)
+        lay_join(tick, 2)
+        side = matmul(joined, 1, most, 2, depth)
+        lay_join(tick, 0)
+        summed = side + matmul(joined, 0, most)
+        settle(current, jnp.where(summed >= 0, summed, 0.1 * summed))
         rows = most
         for block in range(blocks):
             rows -= 2
-            hidden = matmul(taps_of(current, current_edge, rows), 3 + 2 * block)
-            settle(middle, middle_edge, jnp.maximum(hidden, 0.0), rows)
+            settle(middle, jnp.maximum(matmul(current, 3 + 2 * block, rows), 0.0))
             if block == 0:
                 @pl.when(tick + 1 < ticks)
                 def _():
@@ -238,11 +239,11 @@
                 def _():
                     fetched(tick + 2).start()
             rows -= 2
-            kept = current[2 : 2 + rows].astype(jnp.float32).reshape(rows * groups, wide)
-            added = kept + matmul(taps_of(middle, middle_edge, rows), 4 + 2 * block)
+            kept = current[1 : 1 + rows, :, wide : 2 * wide].astype(jnp.float32)
+            added = kept + matmul(middle, 4 + 2 * block, rows)
             if block + 1 < blocks:
-                settle(current, current_edge, added, rows)
-        deliver[tick] = added.reshape(band_rows, groups, wide).astype(jnp.bfloat16)
+                settle(current, added)
+        deliver[tick] = added.astype(jnp.bfloat16)
 
         @pl.when(tick + 1 < ticks)
         def _():
@@ -303,12 +304,9 @@
         scratch_shapes=[
             vmem((3 + 2 * blocks) * 18 * channels, wide),
             vmem(ticks, 3, band_rows + 2 * rim, groups, wide),
-            vmem(3, band_rows + 2 * rim, groups, LANES),
-            vmem(most, groups, wide),
-            vmem(most, groups, LANES),
-            vmem(most, groups, wide),
-            vmem(most, groups, LANES),
-            pltpu.VMEM((most * groups, wide), jnp.float32),
+            vmem(most, groups, 27 * LANES),
+            vmem(most - 2, groups, 9 * LANES),
+            vmem(most - 4, groups, 9 * LANES),
             vmem(ticks, *state),
             vmem(ticks, *state),
             pltpu.VMEM((ticks, 2, groups, LANES), jnp.int32),

time: 46.7 us -> 46 us (0.985)
  Pallas kernels: 42.6 us -> 41.9 us
    pallas_call x1, Pallas kernels: 42.6 us -> 41.9 us  [shards(): pl.pallas_call(functools.partial(kernel, ticks, blocks, row_count), out_s...]
where the time goes in v3:
time: 46 us; the launch traced here: 45.8 us
  Pallas kernels  41.9 us (91%)
  local copies, waits for them, and re-layouts  3.84 us (8%)
    pallas_call x1, Pallas kernels, shards(): pl.pallas_call(functools.partial(kernel, ticks, blocks, row_count), out_s...  41.9 us
    unnamed x14, local copies, waits for them, and re-layouts  2.91 us
    reshape x1, local copies, waits for them, and re-layouts, shards(): return result.reshape(ticks, band_rows, line)  0.93 us

profile of v3, /device:TPU:0, one launch (start us, length us, event | category | flops | bytes accessed | tf_op | source)
XLA Modules:
  0.0 45.8 jit_solution(10585458814158458535)
XLA Ops:
  0.0 0.0 copy-start.2
  0.0 1.0 %copy.14 = bf16[2,8,32,256]{3,2,1,0:T(8,128)(2,1)S(1)} copy(bf16[2,8,32,256]{3,1,2,0:T(8,128)(2,1)} %bitcast.17) | data formatting | bytes 524288
  1.1 0.0 copy-done.2
  1.1 0.0 copy-start.4
  1.1 0.1 copy.13
  1.2 0.0 copy-start.3
  1.2 0.8 %copy-done.4 = bf16[3,576,64]{1,2,0:T(8,128)(2,1)S(1)} copy-done((bf16[3,576,64]{1,2,0:T(8,128)(2,1)S(1)}, bf16[3,576,64]{1,2,0:T(8,128)(2,1)}, u32[]{:S(2)}) %copy-start.4) | copy-done | bytes 221208
  2.0 0.2 copy.7.join_w
  2.3 0.0 copy-done.3
  2.3 0.0 copy-start
  2.3 0.0 copy-start.1
  2.3 0.3 copy.8.res_w
  2.6 0.4 copy-done
  3.0 0.0 copy-done.1
  3.0 41.9 %shard_map.64 = bf16[3,8,32,256]{3,2,1,0:T(8,128)(2,1)S(1)} custom-call(bf16[3,8,32,256]{3,2,1,0:T(8,128)(2,1)S(1)} %copy.13, bf16[2,8,32,256]{3,2,1,0:T(8,128)(2,1)S(1)} %copy.14, s32[1,2,3]{2,1,0:T(2,128)S(1)} %bitcast.15, s32[4]{0:T(128)S(1)} %copy-done.1, bf16[3,576,64]{2,1,0:T(8,128)(2,1)S(1)} %copy.7.join_w, bf16[4,3,192,64]{3,2,1,0:T(8,128)(2,1)S(1)} %copy.8.res_w), custom_call_target="tpu_custom_call" | custom-call | tf_op jit(solution)/shard_map/pallas_call | solution.py:299
  44.9 0.9 %reshape.11 = bf16[3,8,8192]{2,1,0:T(8,128)(2,1)} reshape(bf16[3,8,32,256]{3,2,1,0:T(8,128)(2,1)S(1)} %shard_map.64) | data formatting | bytes 786432 | tf_op jit(solution)/shard_map/reshape | solution.py:328
Async XLA Ops:
  0.0 1.1 %copy-start.2 = (bf16[3,8,8192]{2,1,0:T(8,128)(2,1)S(1)}, bf16[3,8,8192]{2,1,0:T(8,128)(2,1)}, u32[]{:S(2)}) copy-start(bf16[3,8,8192]{2,1,0:T(8,128)(2,1)} %param.6) | copy-start | bytes 1179652
  1.1 0.9 %copy-start.4 = (bf16[3,576,64]{1,2,0:T(8,128)(2,1)S(1)}, bf16[3,576,64]{1,2,0:T(8,128)(2,1)}, u32[]{:S(2)}) copy-start(bf16[3,576,64]{1,2,0:T(8,128)(2,1)} %param.10) | copy-start | bytes 663556
  1.2 1.1 %copy-start.3 = (bf16[4,3,192,64]{2,3,1,0:T(8,128)(2,1)S(1)}, bf16[4,3,192,64]{2,3,1,0:T(8,128)(2,1)}, u32[]{:S(2)}) copy-start(bf16[4,3,192,64]{2,3,1,0:T(8,128)(2,1)} %param.11) | copy-start | bytes 884740
  2.3 0.7 %copy-start = (s32[3,1,2]{0,2,1:T(2,128)S(1)}, s32[3,1,2]{0,2,1:T(2,128)}, u32[]{:S(2)}) copy-start(s32[3,1,2]{0,2,1:T(2,128)} %param.8) | copy-start | bytes 76
  2.3 0.7 %copy-start.1 = (s32[4]{0:T(128)S(1)}, s32[4]{0:T(128)}, u32[]{:S(2)}) copy-start(s32[4]{0:T(128)} %clip.1) | copy-start | bytes 52

commit v4 on v3

--- a/solution.py
+++ b/solution.py
@@ -8,7 +8,7 @@
 from jax.sharding import PartitionSpec as P
 
 SECTIONS = 4
-MAXSHIFT = 8
+PIECES = 4
 LANES = 128
 
 
@@ -123,23 +123,48 @@
         )
 
     def send_halo(tick, slot):
-        for copy in halo(tick, slot):
-            copy.start()
+        down, up = halo(tick, slot)
+        pl.when(band < band_count - 1)(down.start)
+        pl.when(band > 0)(up.start)
+
+    def await_halo(tick, slot):
+        from_above, from_below = halo(tick, slot)
+        pl.when(band > 0)(from_above.wait_recv)
+        pl.when(band < band_count - 1)(from_below.wait_recv)
+
+    def finish_halo(tick, slot):
+        down, up = halo(tick, slot)
+        pl.when(band < band_count - 1)(down.wait_send)
+        pl.when(band > 0)(up.wait_send)
 
     def backwards(tick):
         return row_count - band_count * tick
 
+    piece = band_rows // PIECES
+
     def fetched(tick):
-        return copy_of(feat.at[tick], grown.at[tick, 2, own], feat_send.at[tick],
-                       feat_recv.at[tick], backwards(tick))
+        return [
+            copy_of(feat.at[tick, pl.ds(part * piece, piece)],
+                    grown.at[tick, 2, pl.ds(rim + part * piece, piece)],
+                    feat_send.at[tick, part], feat_recv.at[tick, part], backwards(tick))
+            for part in range(PIECES)
+        ]
+
+    def fetch(tick):
+        for copy in fetched(tick):
+            copy.start()
 
     def shifts(tick):
         return copy_of(shift_out.at[tick], shift_in.at[tick], flow_send.at[tick],
                        flow_recv.at[tick], backwards(tick))
 
     def delivered(tick):
-        return copy_of(deliver.at[tick], out.at[tick], out_send.at[tick], out_recv.at[tick],
-                       band_count * tick)
+        return [
+            copy_of(deliver.at[tick, pl.ds(part * piece, piece)],
+                    out.at[tick, pl.ds(part * piece, piece)],
+                    out_send.at[tick, part], out_recv.at[tick, part], band_count * tick)
+            for part in range(PIECES)
+        ]
 
     home = pltpu.make_async_copy(deliver.at[0], out.at[0], local_sem)
 
@@ -184,9 +209,6 @@
                 band_w[base + start : base + start + channels, 0:LANES] = left_part
                 band_w[base + start : base + start + channels, LANES : 2 * LANES] = right_part
 
-    if ticks > 1:
-        fetched(1).start()
-
     def matmul(left, layer, rows, slots=1, start=0):
         return jnp.dot(
             left[0:rows, :, start : start + slots * depth].reshape(rows * groups, slots * depth),
@@ -207,8 +229,7 @@
     most = band_rows + 2 * rim - 2
 
     def lay_join(tick, slot):
-        for copy in halo(tick, slot):
-            copy.wait_recv()
+        await_halo(tick, slot)
         lay_taps(joined, framed(grown[tick, slot].astype(jnp.float32), rim), slot * depth)
 
     def one_tick(tick, nothing):
@@ -216,6 +237,8 @@
         lay_join(tick, 2)
         side = matmul(joined, 1, most, 2, depth)
         lay_join(tick, 0)
+        if ticks > 1:
+            pl.when(tick == 0)(lambda: fetch(1))
         summed = side + matmul(joined, 0, most)
         settle(current, jnp.where(summed >= 0, summed, 0.1 * summed))
         rows = most
@@ -229,15 +252,16 @@
                     earlier = reset(made[tick].astype(jnp.float32), tick + 1)
                     grown[tick + 1, 1, own] = warp(earlier, shift_in[tick + 1, 1])
                     send_halo(tick + 1, 1)
+
+                @pl.when(tick + 2 < ticks)
+                def _():
+                    fetch(tick + 2)
             if block == blocks - 1:
                 @pl.when(tick + 1 < ticks)
                 def _():
-                    fetched(tick + 1).wait_recv()
+                    for copy in fetched(tick + 1):
+                        copy.wait_recv()
                     send_halo(tick + 1, 2)
-
-                @pl.when(tick + 2 < ticks)
-                def _():
-                    fetched(tick + 2).start()
             rows -= 2
             kept = current[1 : 1 + rows, :, wide : 2 * wide].astype(jnp.float32)
             added = kept + matmul(middle, 4 + 2 * block, rows)
@@ -258,7 +282,8 @@
 
         @pl.when(tick > 0)
         def _():
-            delivered(tick).start()
+            for copy in delivered(tick):
+                copy.start()
 
         return nothing
 
@@ -267,13 +292,14 @@
     home.wait()
     for tick in range(ticks):
         for slot in range(3):
-            for copy in halo(tick, slot):
-                copy.wait_send()
+            finish_halo(tick, slot)
         if tick > 0:
             shifts(tick).wait_send()
-            fetched(tick).wait_send()
-            delivered(tick).wait_send()
-            delivered(tick).wait_recv()
+            for copy in fetched(tick):
+                copy.wait_send()
+            for copy in delivered(tick):
+                copy.wait_send()
+                copy.wait_recv()
 
 
 def shards(features, carried, flow_shift, clip_start, join_weight, res_weight):
@@ -313,12 +339,12 @@
             pltpu.VMEM((ticks, 2, groups, LANES), jnp.int32),
             dma((ticks, 3, 2)),
             dma((ticks, 3, 2)),
+            dma((ticks, PIECES)),
+            dma((ticks, PIECES)),
             dma((ticks,)),
             dma((ticks,)),
-            dma((ticks,)),
-            dma((ticks,)),
-            dma((ticks,)),
-            dma((ticks,)),
+            dma((ticks, PIECES)),
+            dma((ticks, PIECES)),
             dma,
         ],
         compiler_params=pltpu.CompilerParams(

time: 46 us -> 45.4 us (0.987)
  Pallas kernels: 41.9 us -> 41.4 us
    pallas_call x1, Pallas kernels: 41.9 us -> 41.4 us  [shards(): pl.pallas_call(functools.partial(kernel, ticks, blocks, row_count), out_s...]
where the time goes in v4:
time: 45.4 us; the launch traced here: 45.3 us
  Pallas kernels  41.4 us (91%)
  local copies, waits for them, and re-layouts  3.84 us (8%)
    pallas_call x1, Pallas kernels, shards(): pl.pallas_call(functools.partial(kernel, ticks, blocks, row_count), out_s...  41.4 us
    unnamed x14, local copies, waits for them, and re-layouts  2.91 us
    reshape x1, local copies, waits for them, and re-layouts, shards(): return result.reshape(ticks, band_rows, line)  0.93 us

profile of v4, /device:TPU:0, one launch (start us, length us, event | category | flops | bytes accessed | tf_op | source)
XLA Modules:
  0.0 45.3 jit_solution(2164193619499166579)
XLA Ops:
  0.0 0.0 copy-start.2
  0.0 1.0 %copy.14 = bf16[2,8,32,256]{3,2,1,0:T(8,128)(2,1)S(1)} copy(bf16[2,8,32,256]{3,1,2,0:T(8,128)(2,1)} %bitcast.17) | data formatting | bytes 524288
  1.1 0.0 copy-done.2
  1.1 0.0 copy-start.4
  1.1 0.1 copy.13
  1.2 0.0 copy-start.3
  1.2 0.8 %copy-done.4 = bf16[3,576,64]{1,2,0:T(8,128)(2,1)S(1)} copy-done((bf16[3,576,64]{1,2,0:T(8,128)(2,1)S(1)}, bf16[3,576,64]{1,2,0:T(8,128)(2,1)}, u32[]{:S(2)}) %copy-start.4) | copy-done | bytes 221208
  2.0 0.2 copy.7.join_w
  2.3 0.0 copy-done.3
  2.3 0.0 copy-start
  2.3 0.0 copy-start.1
  2.3 0.3 copy.8.res_w
  2.6 0.4 copy-done
  3.0 0.0 copy-done.1
  3.0 41.4 %shard_map.64 = bf16[3,8,32,256]{3,2,1,0:T(8,128)(2,1)S(1)} custom-call(bf16[3,8,32,256]{3,2,1,0:T(8,128)(2,1)S(1)} %copy.13, bf16[2,8,32,256]{3,2,1,0:T(8,128)(2,1)S(1)} %copy.14, s32[1,2,3]{2,1,0:T(2,128)S(1)} %bitcast.15, s32[4]{0:T(128)S(1)} %copy-done.1, bf16[3,576,64]{2,1,0:T(8,128)(2,1)S(1)} %copy.7.join_w, bf16[4,3,192,64]{3,2,1,0:T(8,128)(2,1)S(1)} %copy.8.res_w), custom_call_target="tpu_custom_call" | custom-call | tf_op jit(solution)/shard_map/pallas_call | solution.py:325
  44.3 0.9 %reshape.11 = bf16[3,8,8192]{2,1,0:T(8,128)(2,1)} reshape(bf16[3,8,32,256]{3,2,1,0:T(8,128)(2,1)S(1)} %shard_map.64) | data formatting | bytes 786432 | tf_op jit(solution)/shard_map/reshape | solution.py:354
Async XLA Ops:
  0.0 1.1 %copy-start.2 = (bf16[3,8,8192]{2,1,0:T(8,128)(2,1)S(1)}, bf16[3,8,8192]{2,1,0:T(8,128)(2,1)}, u32[]{:S(2)}) copy-start(bf16[3,8,8192]{2,1,0:T(8,128)(2,1)} %param.6) | copy-start | bytes 1179652
  1.1 0.9 %copy-start.4 = (bf16[3,576,64]{1,2,0:T(8,128)(2,1)S(1)}, bf16[3,576,64]{1,2,0:T(8,128)(2,1)}, u32[]{:S(2)}) copy-start(bf16[3,576,64]{1,2,0:T(8,128)(2,1)} %param.10) | copy-start | bytes 663556
  1.2 1.1 %copy-start.3 = (bf16[4,3,192,64]{2,3,1,0:T(8,128)(2,1)S(1)}, bf16[4,3,192,64]{2,3,1,0:T(8,128)(2,1)}, u32[]{:S(2)}) copy-start(bf16[4,3,192,64]{2,3,1,0:T(8,128)(2,1)} %param.11) | copy-start | bytes 884740
  2.3 0.7 %copy-start = (s32[3,1,2]{0,2,1:T(2,128)S(1)}, s32[3,1,2]{0,2,1:T(2,128)}, u32[]{:S(2)}) copy-start(s32[3,1,2]{0,2,1:T(2,128)} %param.8) | copy-start | bytes 76
  2.3 0.7 %copy-start.1 = (s32[4]{0:T(128)S(1)}, s32[4]{0:T(128)}, u32[]{:S(2)}) copy-start(s32[4]{0:T(128)} %clip.1) | copy-start | bytes 52

commit v5 on v4

--- a/solution.py
+++ b/solution.py
@@ -80,13 +80,13 @@
 
 
 def kernel(
-    ticks, blocks, row_count, feat, carried, flow, clip, join_w, res_w, out,
-    band_w, grown, joined, current, middle, made,
+    ticks, blocks, row_count, feat, carried, flow, clip, join_stored, res_stored, out,
+    join_w, res_w, band_w, grown, joined, current, middle, made,
     deliver, shift_out, shift_in,
-    halo_send, halo_recv, feat_send, feat_recv, flow_send, flow_recv, out_send, out_recv, local_sem,
+    halo_send, halo_recv, feat_send, feat_recv, flow_send, flow_recv, out_send, out_recv, local_sem, join_sem, res_sem,
 ):
     band_rows, groups, wide = feat.shape[1:]
-    channels = join_w.shape[2]
+    channels = join_w.shape[1]
     rim = 1 + 2 * blocks
     own = pl.ds(rim, band_rows)
     band_count = row_count // SECTIONS
@@ -101,6 +101,10 @@
     offsets = {1, row_count - 1}
     for tick in range(1, ticks):
         offsets |= {(band_count * tick) % row_count, (-band_count * tick) % row_count}
+    join_load = pltpu.make_async_copy(join_stored, join_w, join_sem)
+    res_load = pltpu.make_async_copy(res_stored, res_w, res_sem)
+    join_load.start()
+    res_load.start()
     barrier = pltpu.get_barrier_semaphore()
     for offset in sorted(offsets):
         pl.semaphore_signal(
@@ -190,17 +194,22 @@
         shifts(tick).start()
 
     depth = 18 * channels
+    join_load.wait()
+    res_load.wait()
     for layer in range(3 + 2 * blocks):
         base = layer * depth
         for kernel_row in range(3):
-            taps = []
-            for column in range(3):
-                if layer < 3:
-                    start = (column * 3 + layer) * channels
-                    taps.append(join_w[kernel_row, start : start + channels, :])
-                else:
-                    start = column * channels
-                    taps.append(res_w[layer - 3, kernel_row, start : start + channels, :])
+            if layer < 3:
+                stored = [
+                    join_w[kernel_row, :, (column * 3 + layer) * channels : (column * 3 + layer + 1) * channels]
+                    for column in range(3)
+                ]
+            else:
+                stored = [
+                    res_w[layer - 3, kernel_row, :, column * channels : (column + 1) * channels]
+                    for column in range(3)
+                ]
+            taps = [tap.astype(jnp.float32).T.astype(jnp.bfloat16) for tap in stored]
             for index, (left_part, right_part) in enumerate(band_blocks(taps)):
                 if index < 4:
                     start = (kernel_row * 4 + index) * channels
@@ -319,15 +328,18 @@
         return pltpu.VMEM(shape, jnp.bfloat16)
 
     whole = pl.BlockSpec(memory_space=pltpu.VMEM)
+    stored = pl.BlockSpec(memory_space=pl.ANY)
     scalars = pl.BlockSpec(memory_space=pltpu.SMEM)
     state = (band_rows, groups, wide)
     dma = pltpu.SemaphoreType.DMA
     result = pl.pallas_call(
         functools.partial(kernel, ticks, blocks, row_count),
         out_shape=jax.ShapeDtypeStruct((ticks, *state), jnp.bfloat16),
-        in_specs=[whole, whole, scalars, scalars, whole, whole],
+        in_specs=[whole, whole, scalars, scalars, stored, stored],
         out_specs=pl.BlockSpec(memory_space=pl.ANY),
         scratch_shapes=[
+            vmem(*join_weight.transpose(0, 2, 1).shape),
+            vmem(*res_weight.transpose(0, 1, 3, 2).shape),
             vmem((3 + 2 * blocks) * 18 * channels, wide),
             vmem(ticks, 3, band_rows + 2 * rim, groups, wide),
             vmem(most, groups, 27 * LANES),
@@ -346,11 +358,16 @@
             dma((ticks, PIECES)),
             dma((ticks, PIECES)),
             dma,
+            dma,
+            dma,
         ],
         compiler_params=pltpu.CompilerParams(
             collective_id=0, has_side_effects=True, vmem_limit_bytes=48 * 1024 * 1024
         ),
-    )(grouped(features), grouped(carried), flow_shift.transpose(1, 2, 0), clip_start, join_weight, res_weight)
+    )(
+        grouped(features), grouped(carried), flow_shift.transpose(1, 2, 0), clip_start,
+        join_weight.transpose(0, 2, 1), res_weight.transpose(0, 1, 3, 2),
+    )
     return result.reshape(ticks, band_rows, line)
 
 

time: 45.4 us -> 45.7 us (level)
  Pallas kernels: 41.4 us -> 42.5 us
  local copies, waits for them, and re-layouts: 3.84 us -> 3.03 us
    pallas_call x1, Pallas kernels: 41.4 us -> 42.5 us  [shards(): pl.pallas_call(functools.partial(kernel, ticks, blocks, row_count), out_s...]
    unnamed x14 -> x12, local copies, waits for them, and re-layouts: 2.91 us -> 2.1 us
where the time goes in v5:
time: 45.7 us; the launch traced here: 45.6 us
  Pallas kernels  42.5 us (93%)
  local copies, waits for them, and re-layouts  3.03 us (7%)
    pallas_call x1, Pallas kernels, shards(): pl.pallas_call(functools.partial(kernel, ticks, blocks, row_count), out_s...  42.5 us
    unnamed x12, local copies, waits for them, and re-layouts  2.1 us
    reshape x1, local copies, waits for them, and re-layouts, shards(): return result.reshape(ticks, band_rows, line)  0.93 us

profile of v5, /device:TPU:0, one launch (start us, length us, event | category | flops | bytes accessed | tf_op | source)
XLA Modules:
  0.0 45.6 jit_solution(9511378731345542777)
XLA Ops:
  0.0 0.0 copy-start.4
  0.0 1.0 %copy.12 = bf16[2,8,32,256]{3,2,1,0:T(8,128)(2,1)S(1)} copy(bf16[2,8,32,256]{3,1,2,0:T(8,128)(2,1)} %bitcast.21) | data formatting | bytes 524288
  1.1 0.0 copy-done.4
  1.1 0.0 copy-start
  1.1 0.0 copy-start.1
  1.1 0.1 copy.11
  1.2 0.0 copy-start.2
  1.2 0.0 copy-start.3
  1.2 0.9 %copy-done = bf16[4,3,192,64]{2,3,1,0:T(8,128)(2,1)S(1)} copy-done((bf16[4,3,192,64]{2,3,1,0:T(8,128)(2,1)S(1)}, bf16[4,3,192,64]{2,3,1,0:T(8,128)(2,1)}, u32[]{:S(2)}) %copy-start) | copy-done | bytes 294936
  2.1 0.1 copy-done.1
  2.1 0.0 copy-done.2
  2.1 0.0 copy-done.3
  2.1 42.5 %shard_map.64 = bf16[3,8,32,256]{3,2,1,0:T(8,128)(2,1)S(1)} custom-call(bf16[3,8,32,256]{3,2,1,0:T(8,128)(2,1)S(1)} %copy.11, bf16[2,8,32,256]{3,2,1,0:T(8,128)(2,1)S(1)} %copy.12, s32[1,2,3]{2,1,0:T(2,128)S(1)} %bitcast.19, s32[4]{0:T(128)S(1)} %copy-done.3, bf16[3,64,576]{2,1,0:T(8,128)(2,1)S(1)} %bitcast.18, bf16[4,3,64,192]{3,2,1,0:T(8,128)(2,1)S(1)} %bitcast.17), custom_call_target="tpu_custom_call" | custom-call | tf_op jit(solution)/shard_map/pallas_call | solution.py:335
  44.6 0.9 %reshape.11 = bf16[3,8,8192]{2,1,0:T(8,128)(2,1)} reshape(bf16[3,8,32,256]{3,2,1,0:T(8,128)(2,1)S(1)} %shard_map.64) | data formatting | bytes 786432 | tf_op jit(solution)/shard_map/reshape | solution.py:371
Async XLA Ops:
  0.0 1.1 %copy-start.4 = (bf16[3,8,8192]{2,1,0:T(8,128)(2,1)S(1)}, bf16[3,8,8192]{2,1,0:T(8,128)(2,1)}, u32[]{:S(2)}) copy-start(bf16[3,8,8192]{2,1,0:T(8,128)(2,1)} %param.6) | copy-start | bytes 1179652
  1.1 1.0 %copy-start = (bf16[4,3,192,64]{2,3,1,0:T(8,128)(2,1)S(1)}, bf16[4,3,192,64]{2,3,1,0:T(8,128)(2,1)}, u32[]{:S(2)}) copy-start(bf16[4,3,192,64]{2,3,1,0:T(8,128)(2,1)} %param.11) | copy-start | bytes 884740
  1.1 1.1 %copy-start.1 = (bf16[3,576,64]{1,2,0:T(8,128)(2,1)S(1)}, bf16[3,576,64]{1,2,0:T(8,128)(2,1)}, u32[]{:S(2)}) copy-start(bf16[3,576,64]{1,2,0:T(8,128)(2,1)} %param.10) | copy-start | bytes 663556
  1.2 1.0 %copy-start.2 = (s32[3,1,2]{0,2,1:T(2,128)S(1)}, s32[3,1,2]{0,2,1:T(2,128)}, u32[]{:S(2)}) copy-start(s32[3,1,2]{0,2,1:T(2,128)} %param.8) | copy-start | bytes 76
  1.2 1.0 %copy-start.3 = (s32[4]{0:T(128)S(1)}, s32[4]{0:T(128)}, u32[]{:S(2)}) copy-start(s32[4]{0:T(128)} %clip.1) | copy-start | bytes 52
